TPU v7x, 256 devices: a whole 4x4x8 slice. The times are simulated.
256 devices in a mesh: dp: 64 (over y_hi, z, x), mp: 4 (over y_lo, core).
Axes of the slice: x: 4, y: 4 (y_hi: 2, y_lo: 2; y = y_hi * 2 + y_lo), z: 8, core: 2. Of those that a mesh axis runs over, the one named last changes fastest.
Arguments:
- image_emb: bfloat16 [65536, 1024], P('dp', 'mp'), may hold values from -1 to 1
- text_emb: bfloat16 [65536, 1024], P('dp', 'mp'), may hold values from -1 to 1
- logit_scale: float32 [1], replicated, may hold values from 60 to 100
Outputs:
- image_grad: bfloat16 [65536, 1024], P('dp', 'mp')
- text_grad: bfloat16 [65536, 1024], P('dp', 'mp')
- pair_loss: float32 [65536], P(('dp', 'mp'))
All inputs are finite; a program needn't handle non-finite values.
Results may differ from a plain program's by a relative error of at most 0.0041.
Values may be sent and summed in bfloat16 or wider, within the bound.
A program may use at most 64 MiB of HBM per device.

v0:
```python
import jax
import jax.numpy as jnp
from jax import lax
from jax.sharding import PartitionSpec as P


def shifted(x, axis, by):
    devices = lax.axis_size(axis)
    return lax.ppermute(x, axis, [(i, (i + by) % devices) for i in range(devices)])


def with_halo(cells, sides, width):
    for axis, dim in sides:
        count = lax.axis_size(axis)
        head = lax.slice_in_dim(cells, 0, width, axis=dim)
        tail = lax.slice_in_dim(cells, cells.shape[dim] - width, cells.shape[dim], axis=dim)
        cells = jnp.concatenate(
            [
                lax.ppermute(tail, axis, [(i, (i + 1) % count) for i in range(count)]),
                cells,
                lax.ppermute(head, axis, [((i + 1) % count, i) for i in range(count)]),
            ],
            axis=dim,
        )
    return cells


def contract_width(left_rows, right_rows):
    return lax.dot_general(
        left_rows, right_rows, (((1,), (1,)), ((), ())), preferred_element_type=jnp.float32
    )


def contract_rows(left_rows, right_rows):
    return lax.dot_general(
        left_rows, right_rows, (((0,), (0,)), ((), ())), preferred_element_type=jnp.float32
    )


def row_logsumexp(score_own, score_prev):
    highest = jnp.maximum(jnp.max(score_own, axis=1), jnp.max(score_prev, axis=1))
    summed_exp = jnp.sum(jnp.exp(score_own - highest[:, None]), axis=1) + jnp.sum(
        jnp.exp(score_prev - highest[:, None]), axis=1
    )
    return highest + jnp.log(summed_exp)


def column_logsumexp(scores):
    highest = jnp.max(scores, axis=0)
    return highest + jnp.log(jnp.sum(jnp.exp(scores - highest[None, :]), axis=0))


def add_logs(first_log, second_log):
    highest = jnp.maximum(first_log, second_log)
    return highest + jnp.log(jnp.exp(first_log - highest) + jnp.exp(second_log - highest))


def local(image_emb, text_emb, logit_scale):
    factor = logit_scale[0]
    block_rows = image_emb.shape[0]
    share_rows = block_rows // lax.axis_size("mp")
    row_start = lax.axis_index("mp") * share_rows
    prev_text = shifted(text_emb, "dp", 1)
    own_sum, prev_sum = lax.psum(
        (contract_width(image_emb, text_emb), contract_width(image_emb, prev_text)), "mp"
    )
    score_own = factor * own_sum
    score_prev = factor * prev_sum
    height = score_own.shape[0]
    row_lse = row_logsumexp(score_own, score_prev)
    columns = jnp.stack([column_logsumexp(score_prev), column_logsumexp(score_own)])
    padded = with_halo(columns, (("dp", 0),), 1)
    col_own = add_logs(columns[1], padded[3])
    col_prev = add_logs(padded[0], columns[0])
    row_index = lax.broadcasted_iota(jnp.int32, (height, block_rows), 0)
    col_index = lax.broadcasted_iota(jnp.int32, (height, block_rows), 1)
    identity = (row_index == col_index).astype(jnp.float32)
    diagonal = jnp.sum(score_own * identity, axis=1)
    pair_all = 0.5 * (row_lse + col_own) - diagonal
    pair_loss = lax.dynamic_slice_in_dim(pair_all, row_start, share_rows)
    prob_own = (
        0.5 * (jnp.exp(score_own - row_lse[:, None]) + jnp.exp(score_own - col_own[None, :]))
        - identity
    ).astype(jnp.bfloat16)
    prob_prev = (
        0.5 * (jnp.exp(score_prev - row_lse[:, None]) + jnp.exp(score_prev - col_prev[None, :]))
    ).astype(jnp.bfloat16)
    visit_term = contract_rows(prob_prev, image_emb)
    returned = shifted(visit_term, "dp", -1)
    image_grad = (
        factor
        * (
            jnp.dot(prob_own, text_emb, preferred_element_type=jnp.float32)
            + jnp.dot(prob_prev, prev_text, preferred_element_type=jnp.float32)
        )
    ).astype(jnp.bfloat16)
    own_term = contract_rows(prob_own, image_emb)
    text_grad = (factor * (own_term + returned)).astype(jnp.bfloat16)
    return (image_grad, text_grad, pair_loss)


def solution(mesh):
    return jax.shard_map(
        local,
        mesh=mesh,
        in_specs=(P("dp", "mp"), P("dp", "mp"), P()),
        out_specs=(P("dp", "mp"), P("dp", "mp"), P(("dp", "mp"))),
        check_vma=False,
    )
```

profile of v0, /device:TPU:8, one launch (start us, length us, event | category | flops | bytes accessed | tf_op | source)
XLA Modules:
  0.0 260.6 jit_solution(16301255796070717651)
XLA Ops:
  7.2 0.0 copy-start
  7.2 0.0 all-reduce.3.cloned.1.call-start
  7.2 1.6 collective-permute-start
  8.8 0.0 copy-done
  8.8 3.8 %fusion.5 = f32[1024,1024]{1,0:T(8,128)} fusion(bf16[1024,256]{1,0:T(8,128)(2,1)S(1)} %copy-done, bf16[1024,256]{1,0:T(8,128)(2,1)} %param.4), kind=kOutput, calls=%fused_computation.28 | convolution fusion | flops 536870912 | bytes 5242880 | tf_op jit(solution)/shard_map/dot_general | solution.py:29
  12.6 16.6 %collective-permute-done = bf16[1024,256]{1,0:T(8,128)(2,1)S(1)} collective-permute-done((bf16[1024,256]{1,0:T(8,128)(2,1)}, bf16[1024,256]{1,0:T(8,128)(2,1)S(1)}, u32[]{:S(2)}, u32[]{:S(2)}) %collective-permute-start) | collective-permute-done | bytes 524320 | tf_op jit(solution)/shard_map/ppermute | solution.py:9
  29.2 0.0 copy-start.5
  29.2 0.8 copy-done.5
  30.0 2.7 %fusion.6 = f32[1024,1024]{1,0:T(8,128)} fusion(bf16[1024,256]{1,0:T(8,128)(2,1)S(1)} %copy-done, bf16[1024,256]{1,0:T(8,128)(2,1)S(1)} %collective-permute-done), kind=kOutput, calls=%fused_computation.29 | convolution fusion | flops 536870912 | bytes 5242880 | tf_op jit(solution)/shard_map/dot_general | solution.py:29
  32.7 0.0 all-reduce.3.cloned.1.call-update
  33.4 157.8 %all-reduce.3.cloned.1.call-done = (f32[1024,1024]{1,0:T(8,128)}, f32[1024,1024]{1,0:T(8,128)}) async-done(((f32[1024,1024]{1,0:T(8,128)}, f32[1024,1024]{1,0:T(8,128)}), (f32[1024,1024]{1,0:T(8,128)}, f32[1024,1024]{1,0:T(8,128)})) %all-reduce.3.cloned.1.call-update) | async-done | bytes 8388624 | tf_op jit(solution)/shard_map/psum | solution.py:64
  191.2 0.0 copy-start.1
  191.2 0.0 copy-start.2
  191.2 4.2 %multiply_reduce_fusion.1 = (f32[1024]{0:T(1024)S(1)}, f32[1024]{0:T(1024)S(1)}) fusion(f32[1024,1024]{1,0:T(8,128)} %get-tuple-element.11, f32[]{:T(128)} %bitcast.22, f32[1024,1024]{1,0:T(8,128)} %get-tuple-element.10), kind=kLoop, calls=%fused_computation.9 | loop fusion | flops 4192256 | bytes 8396804 | tf_op jit(solution)/shard_map/reduce_max | solution.py:41
  195.5 0.4 copy-done.1
  195.9 1.3 copy-done.2
  197.2 3.4 %select_reduce_fusion = (f32[1024]{0:T(1024)S(1)}, f32[1024]{0:T(1024)S(1)}, f32[1024]{0:T(1024)S(1)}, f32[1024]{0:T(1024)S(1)}, f32[1024]{0:T(1024)S(1)}) fusion(f32[1024,1024]{1,0:T(8,128)S(1)} %copy-done.1, f32[]{:T(128)} %bitcast.21, f32[1024]{0:T(1024)S(1)} %max.20, f32[1024,1024]{1,0:T(8,128)S(1)} %copy-done.2), kind=kLoop, calls=%fused_computation | loop fusion | flops 11529216 | bytes 8413188 | tf_op jit(solution)/shard_map/reduce_sum | solution.py:78
  200.5 0.7 exponential_reduce_fusion
  201.3 8.1 %collective-permute-start.1 = (f32[1,1024]{1,0:T(1,128)S(1)}, f32[1,1024]{1,0:T(1,128)S(1)}, u32[]{:S(2)}, u32[]{:S(2)}) collective-permute-start(f32[1,1024]{1,0:T(1,128)S(1)} %bitcast.27), channel_id=1, source_target_pairs={{4,0},{8,4},{12,8},{16,12},{20,16},{24,20},{28,24},{32,28},{36,32}... | collective-permute-start | bytes 12296 | tf_op jit(solution)/shard_map/ppermute | solution.py:21
  209.4 0.7 exponential_reduce_fusion.1
  210.1 0.6 collective-permute-done.1
  210.8 0.1 collective-permute-start.2
  210.9 9.5 %collective-permute-done.2 = f32[1,1024]{1,0:T(1,128)S(1)} collective-permute-done((f32[1,1024]{1,0:T(1,128)S(1)}, f32[1,1024]{1,0:T(1,128)S(1)}, u32[]{:S(2)}, u32[]{:S(2)}) %collective-permute-start.2) | collective-permute-done | bytes 4128 | tf_op jit(solution)/shard_map/ppermute | solution.py:19
  220.5 3.8 %multiply_convert_fusion = (bf16[1024,1024]{1,0:T(8,128)(2,1)S(1)}, bf16[1024,1024]{1,0:T(8,128)(2,1)S(1)}) fusion(f32[1024,1024]{1,0:T(8,128)S(1)} %copy-done.2, f32[1024]{0:T(1024)S(1)} %bitcast.26, f32[1024]{0:T(1024)S(1)} %get-tuple-element.13, f32[]{:T(128)} %bitcast.24, f32[1024]{0:T(1024)S(1)} %bitcast.25, f32[1024,1024]{1,0:T(8,128)S(1)} %copy-done.1), kind=kLoop, calls=%fused_computation.1 | loop fusion | flops 15728640 | bytes 12595204 | tf_op jit(solution)/shard_map/convert_element_type | solution.py:87
  224.3 0.0 copy-start.3
  224.3 1.3 copy-done.3
  225.6 1.7 fusion.8
  227.4 0.0 copy-start.4
  227.4 2.0 collective-permute-start.3
  229.4 0.6 dynamic_slice.3
  230.0 2.4 fusion.7
  232.4 0.0 copy-done.4
  232.4 1.5 multiply_convert_fusion.1
  233.9 17.0 %collective-permute-done.3 = f32[1024,256]{1,0:T(8,128)} collective-permute-done((f32[1024,256]{1,0:T(8,128)}, f32[1024,256]{1,0:T(8,128)}, u32[]{:S(2)}, u32[]{:S(2)}) %collective-permute-start.3) | collective-permute-done | bytes 1048608 | tf_op jit(solution)/shard_map/ppermute | solution.py:9
  251.0 2.8 %fusion.1 = bf16[1024,256]{1,0:T(8,128)(2,1)} fusion(f32[1024,256]{1,0:T(8,128)} %collective-permute-done.3, bf16[1024,1024]{1,0:T(8,128)(2,1)S(1)} %get-tuple-element.16, bf16[1024,256]{1,0:T(8,128)(2,1)S(1)} %copy-done, f32[]{:T(128)} %bitcast.20), kind=kOutput, calls=%fused_computation.14 | convolution fusion | flops 537657344 | bytes 4194308 | tf_op jit(solution)/shard_map/dot_general | solution.py:35
  (5 shorter events, 0.1 us)
Async XLA Ops:
  7.2 1.6 copy-start
  7.2 184.1 %all-reduce.3.cloned.1.call-start = ((), (), s32[]{:S(2)}) async-start(), calls=%async_computation | async-start | bytes 16777216 | tf_op jit(solution)/shard_map/psum | solution.py:64
  7.2 22.0 %collective-permute-start = (bf16[1024,256]{1,0:T(8,128)(2,1)}, bf16[1024,256]{1,0:T(8,128)(2,1)S(1)}, u32[]{:S(2)}, u32[]{:S(2)}) collective-permute-start(bf16[1024,256]{1,0:T(8,128)(2,1)} %param.4), channel_id=1, source_target_pairs={{0,4},{4,8},{8,12},{12,16},{16,20},{20,24},{24,28},{28,32},{32,36}... | collective-permute-start | bytes 1572872 | tf_op jit(solution)/shard_map/ppermute | solution.py:9
  29.2 0.8 copy-start.5
  191.2 4.6 %copy-start.1 = (f32[1024,1024]{1,0:T(8,128)S(1)}, f32[1024,1024]{1,0:T(8,128)}, u32[]{:S(2)}) copy-start(f32[1024,1024]{1,0:T(8,128)} %get-tuple-element.10) | copy-start | bytes 12582916
  191.2 5.9 %copy-start.2 = (f32[1024,1024]{1,0:T(8,128)S(1)}, f32[1024,1024]{1,0:T(8,128)}, u32[]{:S(2)}) copy-start(f32[1024,1024]{1,0:T(8,128)} %get-tuple-element.11) | copy-start | bytes 12582916
  201.3 9.5 %collective-permute-start.1 = (f32[1,1024]{1,0:T(1,128)S(1)}, f32[1,1024]{1,0:T(1,128)S(1)}, u32[]{:S(2)}, u32[]{:S(2)}) collective-permute-start(f32[1,1024]{1,0:T(1,128)S(1)} %bitcast.27), channel_id=1, source_target_pairs={{4,0},{8,4},{12,8},{16,12},{20,16},{24,20},{28,24},{32,28},{36,32}... | collective-permute-start | bytes 12296 | tf_op jit(solution)/shard_map/ppermute | solution.py:21
  210.8 9.7 %collective-permute-start.2 = (f32[1,1024]{1,0:T(1,128)S(1)}, f32[1,1024]{1,0:T(1,128)S(1)}, u32[]{:S(2)}, u32[]{:S(2)}) collective-permute-start(f32[1,1024]{1,0:T(1,128)S(1)} %bitcast.30), channel_id=1, source_target_pairs={{0,4},{4,8},{8,12},{12,16},{16,20},{20,24},{24,28},{28,32},{32,36}... | collective-permute-start | bytes 12296 | tf_op jit(solution)/shard_map/ppermute | solution.py:19
  224.3 1.4 copy-start.3
  227.4 5.0 %copy-start.4 = (bf16[1024,256]{1,0:T(8,128)(2,1)S(1)}, bf16[1024,256]{1,0:T(8,128)(2,1)}, u32[]{:S(2)}) copy-start(bf16[1024,256]{1,0:T(8,128)(2,1)} %param.4) | copy-start | bytes 1572868
  227.4 23.6 %collective-permute-start.3 = (f32[1024,256]{1,0:T(8,128)}, f32[1024,256]{1,0:T(8,128)}, u32[]{:S(2)}, u32[]{:S(2)}) collective-permute-start(f32[1024,256]{1,0:T(8,128)} %fusion.8), channel_id=1, source_target_pairs={{0,252},{4,0},{8,4},{12,8},{16,12},{20,16},{24,20},{28,24},{32,28}... | collective-permute-start | bytes 3145736 | tf_op jit(solution)/shard_map/ppermute | solution.py:9
Sparse Core Ops, SparseCore 0:
  32.9 158.3 all-reduce.2
where the time goes:
time: 261 us
  waiting for transfers between devices  202 us (77%)
  matrix products  14.9 us (6%)
  between operations  14.8 us (6%)
  other arithmetic  13 us (5%)
  starting transfers between devices  11.9 us (5%)
  local copies, waits for them, and re-layouts  4.47 us (2%)
    psum x1, waiting for transfers between devices, local(): lax.psum((contract_width(image_emb, text_emb), contract_width(image_emb,...  158 us
    ppermute x2, waiting for transfers between devices, shifted(): lax.ppermute(x, axis, [(i, (i + by) % devices) for i in range(devices)])  33.7 us
    ppermute x1, waiting for transfers between devices, with_halo(): lax.ppermute(tail, axis, [(i, (i + 1) % count) for i in range(count)])  9.54 us
    ppermute x1, starting transfers between devices, with_halo(): lax.ppermute(head, axis, [((i + 1) % count, i) for i in range(count)])  8.15 us
    dot_general x2, matrix products, contract_width(): lax.dot_general(left_rows, right_rows, (((1,), (1,)), ((), ())), preferre...  6.49 us
  transfers between devices with their start and end apart: 5, of which 5 were waited for; matrix products, arithmetic and copies ran while one was open for 3% of the time, Pallas kernels for 0%

commit v1 on v0

v1 whole, which is shorter than its diff:
```python
import functools

import jax
import jax.numpy as jnp
from jax import lax
from jax.experimental import pallas as pl
from jax.experimental.pallas import tpu as pltpu
from jax.sharding import PartitionSpec as P

MESH = pl.DeviceIdType.MESH
F32 = jnp.float32
BF16 = jnp.bfloat16

Y_T = 0
Y_I = 2
C_I = 6
C_T = 7
X_T = 9
C_P = 13
C_F = 15
S_R = 19
S_C = 22
P_C = 24
V_X = 26
G_Y = 30
T_Y = 34
N_COPIES = 38


def dot_nt(a, b):
    return lax.dot_general(a, b, (((1,), (1,)), ((), ())), preferred_element_type=F32)


def dot_tn(a, b):
    return lax.dot_general(a, b, (((0,), (0,)), ((), ())), preferred_element_type=F32)


def dot_nn(a, b):
    return lax.dot_general(a, b, (((1,), (0,)), ((), ())), preferred_element_type=F32)


def log_add(a, b):
    top = jnp.maximum(a, b)
    return top + jnp.log(jnp.exp(a - top) + jnp.exp(b - top))


def kernel(
    n_dp,
    factor_ref,
    image_ref,
    text_ref,
    image_out,
    text_out,
    loss_out,
    full,
    cat,
    tail,
    row_exp,
    col_exp,
    col_max,
    col_part,
    row_max,
    row_part,
    row_scale,
    diag,
    col_stat,
    col_lse,
    prob,
    visit_out,
    visit_in,
    part_out,
    part_in,
    text_send,
    send_sem,
    recv_sem,
    local_sem,
):
    d = lax.axis_index("dp")
    m = lax.axis_index("mp")
    core = lax.rem(m, 2)
    c_m = m + 1 - 2 * core
    y_m = lax.rem(m + 2, 4)
    z_m = lax.rem(c_m + 2, 4)
    nxt = lax.rem(d + 1, n_dp)
    prv = lax.rem(d + n_dp - 1, n_dp)
    to_c, to_y, to_z = (d, c_m), (d, y_m), (d, z_m)
    to_next, to_prev = (nxt, m), (prv, m)

    def rows(index):
        return pl.ds(pl.multiple_of(index * 256, 256), 256)

    def remote(src, dst, index, device):
        return pltpu.make_async_remote_copy(
            src_ref=src,
            dst_ref=dst,
            send_sem=send_sem.at[index],
            recv_sem=recv_sem.at[index],
            device_id=device,
            device_id_type=MESH,
        )

    own = pl.ds(0, 256)
    via = pl.ds(256, 256)
    locals_ = [
        pltpu.make_async_copy(image_ref, full.at[:, own], local_sem.at[0]),
        pltpu.make_async_copy(text_ref.at[rows(m)], cat.at[pl.ds(512, 256), own], local_sem.at[1]),
        pltpu.make_async_copy(text_ref.at[rows(c_m)], cat.at[pl.ds(768, 256), own], local_sem.at[2]),
    ]
    for copy in locals_:
        copy.start()

    barrier = pltpu.get_barrier_semaphore()
    for device in (to_c, to_y, to_z, to_next, to_prev):
        pl.semaphore_signal(barrier, inc=1, device_id=device, device_id_type=MESH)
    pl.semaphore_wait(barrier, 5)

    y_text = [
        remote(text_ref.at[rows(y_m)], cat.at[pl.ds(512, 256), via], Y_T, to_y),
        remote(text_ref.at[rows(z_m)], cat.at[pl.ds(768, 256), via], Y_T + 1, to_y),
    ]

    def y_image(r):
        return remote(image_ref.at[rows(r)], full.at[rows(r), via], Y_I + r, to_y)

    c_image = remote(image_ref, full.at[:, pl.ds(512, 256)], C_I, to_c)
    c_text = [
        remote(text_ref.at[rows(c_m)], tail.at[1, :, own], C_T, to_c),
        remote(cat.at[pl.ds(768, 256), via], tail.at[1, :, via], C_T + 1, to_c),
    ]
    x_text = [
        remote(text_ref.at[rows(c_m)], cat.at[via, own], X_T, to_next),
        remote(text_ref.at[rows(m)], cat.at[own, own], X_T + 1, to_next),
        remote(cat.at[pl.ds(768, 256), via], cat.at[via, via], X_T + 2, to_next),
        remote(cat.at[pl.ds(512, 256), via], cat.at[own, via], X_T + 3, to_next),
    ]
    c_prev = [
        remote(cat.at[via, own], tail.at[0, :, own], C_P, to_c),
        remote(cat.at[via, via], tail.at[0, :, via], C_P + 1, to_c),
    ]

    def c_forward(r):
        return remote(full.at[rows(r), via], full.at[rows(r), pl.ds(768, 256)], C_F + r, to_c)

    y_text[1].start()
    y_text[0].start()
    x_text[0].start()
    x_text[1].start()
    c_text[0].start()
    c_image.start()
    for r in range(4):
        y_image(r).start()

    y_text[1].wait_recv()
    x_text[2].start()
    c_text[1].start()
    y_text[0].wait_recv()
    x_text[3].start()
    x_text[0].wait_recv()
    c_prev[0].start()
    x_text[2].wait_recv()
    c_prev[1].start()
    for copy in locals_:
        copy.wait()
    c_image.wait_recv()
    c_text[0].wait_recv()
    c_text[1].wait_recv()
    x_text[1].wait_recv()
    x_text[3].wait_recv()
    c_prev[0].wait_recv()
    c_prev[1].wait_recv()

    factor = factor_ref[0]
    eye = lax.broadcasted_iota(jnp.int32, (256, 256), 0) == lax.broadcasted_iota(
        jnp.int32, (256, 256), 1
    )

    def scores(r, carry):
        y_image(r).wait_recv()
        c_forward(r).start()
        c_forward(r).wait_recv()
        left = full[rows(r), 0:512]
        right = full[rows(r), 512:1024]
        prev = factor * (dot_nt(cat[0:256, :], left) + dot_nt(tail[0], right))
        mine = factor * (dot_nt(cat[512:768, :], left) + dot_nt(tail[1], right))
        top = jnp.maximum(
            jnp.max(prev, axis=0, keepdims=True), jnp.max(mine, axis=0, keepdims=True)
        )
        prev_exp = jnp.exp(prev - top)
        mine_exp = jnp.exp(mine - top)
        row_exp[r, 0:256, :] = prev_exp
        row_exp[r, 256:512, :] = mine_exp
        part = top + jnp.log(
            jnp.sum(prev_exp, axis=0, keepdims=True) + jnp.sum(mine_exp, axis=0, keepdims=True)
        )
        for k in range(2):
            lanes = slice(128 * k, 128 * k + 128)
            row_max[pl.ds(2 * r + k, 1), :] = top[:, lanes]
            row_part[0, pl.ds(2 * r + k, 1), :] = part[:, lanes]
        for tile, scored in enumerate((prev, mine)):
            highest = jnp.max(scored, axis=1, keepdims=True)
            scaled = jnp.exp(scored - highest)
            col_exp[r, 256 * tile : 256 * tile + 256, :] = scaled
            col_max[r, 256 * tile : 256 * tile + 256, :] = jnp.broadcast_to(highest, (256, 128))
            total = highest + jnp.log(jnp.sum(scaled, axis=1, keepdims=True))
            for k in range(2):
                piece = jnp.broadcast_to(total[128 * k : 128 * k + 128], (128, 128))
                col_part[r, 2 * tile + k : 2 * tile + k + 1, :] = piece.T[0:1, :]

        @pl.when(r == m)
        def _():
            found = jnp.sum(jnp.where(eye, mine, 0.0), axis=0, keepdims=True)
            for k in range(2):
                diag[k : k + 1, :] = found[:, 128 * k : 128 * k + 128]

        return carry

    lax.fori_loop(0, 4, scores, 0)

    highest = jnp.maximum(
        jnp.maximum(col_part[0, 0:4], col_part[1, 0:4]), jnp.maximum(col_part[2, 0:4], col_part[3, 0:4])
    )
    summed = (
        jnp.exp(col_part[0, 0:4] - highest)
        + jnp.exp(col_part[1, 0:4] - highest)
        + jnp.exp(col_part[2, 0:4] - highest)
        + jnp.exp(col_part[3, 0:4] - highest)
    )
    col_stat[0, 0:4, :] = highest + jnp.log(summed)
    col_stat[0, 4:8, :] = jnp.zeros((4, 128), F32)
    stats = [
        remote(col_stat.at[0], col_stat.at[1], S_C, to_prev),
        remote(col_stat.at[0], col_stat.at[2], S_C + 1, to_next),
        remote(row_part.at[0], row_part.at[1], S_R, to_y),
        remote(row_part.at[0], row_part.at[2], S_R + 1, to_c),
        remote(row_part.at[0], row_part.at[3], S_R + 2, to_z),
    ]
    for copy in stats:
        copy.start()
    for copy in stats:
        copy.wait_recv()

    parts = [row_part[k] for k in range(4)]
    highest = jnp.maximum(jnp.maximum(parts[0], parts[1]), jnp.maximum(parts[2], parts[3]))
    row_lse = highest + jnp.log(
        jnp.exp(parts[0] - highest)
        + jnp.exp(parts[1] - highest)
        + jnp.exp(parts[2] - highest)
        + jnp.exp(parts[3] - highest)
    )
    row_scale[...] = 0.5 * jnp.exp(row_max[...] - row_lse)
    lse_prev = log_add(col_stat[0, 0:2, :], col_stat[2, 2:4, :])
    lse_own = log_add(col_stat[0, 2:4, :], col_stat[1, 0:2, :])
    row_max[...] = row_lse
    loss_out[...] = 0.5 * (row_max[pl.ds(2 * m, 2), :] + lse_own) - diag[...]
    for tile, lse in enumerate((lse_prev, lse_own)):
        for k in range(2):
            at = 256 * tile + 128 * k
            col_lse[at : at + 128, :] = jnp.broadcast_to(lse[k : k + 1, :], (128, 128)).T

    p_copies = [
        remote(prob.at[pl.ds(512 * tile, 256)], prob.at[pl.ds(512 * tile + 256, 256)], P_C + tile, to_c)
        for tile in range(2)
    ]
    for tile in range(2):
        at = slice(256 * tile, 256 * tile + 256)
        for r in range(4):
            scale = 0.5 * jnp.exp(col_max[r, at, :] - col_lse[at, :])
            for k in range(2):
                lanes = slice(128 * k, 128 * k + 128)
                value = (
                    row_exp[r, at, lanes] * row_scale[2 * r + k : 2 * r + k + 1, :]
                    + col_exp[r, at, lanes] * scale
                )
                if tile == 1:
                    value = value - jnp.where(eye[:, lanes] & (m == r), 1.0, 0.0)
                prob[512 * tile : 512 * tile + 256, 256 * r + 128 * k : 256 * r + 128 * k + 128] = (
                    value.astype(BF16)
                )
        p_copies[tile].start()

    def visit(k):
        at = pl.ds(128 * k, 128)
        return remote(visit_out.at[at], visit_in.at[at], V_X + k, to_prev)

    def send_visit(k):
        visit_out[128 * k : 128 * k + 128, :] = dot_nn(
            prob[128 * k : 128 * k + 128, :], full[:, 0:512]
        ).astype(BF16)
        visit(k).start()

    def partial(r):
        return remote(part_out.at[rows(r)], part_in.at[rows(r)], G_Y + r, to_y)

    send_visit(0)
    send_visit(1)
    p_copies[0].wait_recv()
    p_copies[1].wait_recv()
    for r in range(4):
        part_out[256 * r : 256 * r + 256, :] = dot_tn(
            prob[:, 256 * r : 256 * r + 256], cat[:, 256:512]
        ).astype(BF16)
        partial(r).start()
        if r == 0:
            send_visit(2)
            send_visit(3)

    def text_final(k):
        target = rows(m) if k < 2 else rows(c_m)
        return remote(
            text_send.at[pl.ds(128 * k, 128)],
            text_out.at[target].at[pl.ds(128 * (k % 2), 128)],
            T_Y + k,
            to_y,
        )

    for k in range(4):
        own_term = dot_nn(prob[512 + 128 * k : 640 + 128 * k, :], full[:, 0:512])
        visit(k).wait_recv()
        value = factor * (own_term + visit_in[128 * k : 128 * k + 128, :].astype(F32))
        text_send[128 * k : 128 * k + 128, :] = value[:, 256:512].astype(BF16)
        text_final(k).start()
        start = (m if k < 2 else c_m) * 256 + 128 * (k % 2)
        text_out[pl.ds(pl.multiple_of(start, 128), 128), :] = value[:, 0:256].astype(BF16)

    for r in range(4):
        value = dot_tn(prob[:, 256 * r : 256 * r + 256], cat[:, 0:256])
        partial(r).wait_recv()
        image_out[256 * r : 256 * r + 256, :] = (
            factor * (value + part_in[256 * r : 256 * r + 256, :].astype(F32))
        ).astype(BF16)

    for k in range(4):
        text_final(k).wait_recv()
    for copy in y_text + c_text + x_text + c_prev + [c_image] + stats + p_copies:
        copy.wait_send()
    for r in range(4):
        y_image(r).wait_send()
        c_forward(r).wait_send()
        visit(r).wait_send()
        partial(r).wait_send()
        text_final(r).wait_send()


def local(n_dp, image_emb, text_emb, logit_scale):
    vmem = pltpu.VMEM
    image_grad, text_grad, loss = pl.pallas_call(
        functools.partial(kernel, n_dp),
        out_shape=(
            jax.ShapeDtypeStruct((1024, 256), BF16),
            jax.ShapeDtypeStruct((1024, 256), BF16),
            jax.ShapeDtypeStruct((2, 128), F32),
        ),
        in_specs=[
            pl.BlockSpec(memory_space=pltpu.SMEM),
            pl.BlockSpec(memory_space=pl.ANY),
            pl.BlockSpec(memory_space=pl.ANY),
        ],
        out_specs=[pl.BlockSpec(memory_space=vmem)] * 3,
        scratch_shapes=[
            vmem((1024, 1024), BF16),
            vmem((1024, 512), BF16),
            vmem((2, 256, 512), BF16),
            vmem((4, 512, 256), F32),
            vmem((4, 512, 256), F32),
            vmem((4, 512, 128), F32),
            vmem((4, 8, 128), F32),
            vmem((8, 128), F32),
            vmem((4, 8, 128), F32),
            vmem((8, 128), F32),
            vmem((2, 128), F32),
            vmem((3, 8, 128), F32),
            vmem((512, 128), F32),
            vmem((1024, 1024), BF16),
            vmem((512, 512), BF16),
            vmem((512, 512), BF16),
            vmem((1024, 256), BF16),
            vmem((1024, 256), BF16),
            vmem((512, 256), BF16),
            pltpu.SemaphoreType.DMA((N_COPIES,)),
            pltpu.SemaphoreType.DMA((N_COPIES,)),
            pltpu.SemaphoreType.DMA((3,)),
        ],
        compiler_params=pltpu.CompilerParams(
            collective_id=0, has_side_effects=True, vmem_limit_bytes=48 * 1024 * 1024
        ),
        cost_estimate=pl.CostEstimate(
            flops=3 * 2**31, bytes_accessed=2**21, transcendentals=2**20
        ),
    )(logit_scale, image_emb, text_emb)
    return image_grad, text_grad, loss.reshape(256)


def solution(mesh):
    return jax.shard_map(
        functools.partial(local, mesh.shape["dp"]),
        mesh=mesh,
        in_specs=(P("dp", "mp"), P("dp", "mp"), P()),
        out_specs=(P("dp", "mp"), P("dp", "mp"), P(("dp", "mp"))),
        check_vma=False,
    )
```

time: 261 us -> 77.5 us (0.30)
  the two profiles are of different devices: /device:TPU:8 before, /device:TPU:239 now
where the time goes in v1:
time: 77.5 us; the launch traced here: 77.3 us
  Pallas kernels  71.8 us (93%)
  local copies, waits for them, and re-layouts  4.23 us (5%)
  between operations  1.3 us (2%)
    pallas_call x1, Pallas kernels, local(): pl.pallas_call(functools.partial(kernel, n_dp), out_shape=(jax.ShapeDtype...  71.8 us
    unnamed x7, local copies, waits for them, and re-layouts  4.23 us

profile of v1, /device:TPU:239, one launch (start us, length us, event | category | flops | bytes accessed | tf_op | source)
XLA Modules:
  0.0 77.3 jit_solution(664864952109085399)
XLA Ops:
  1.3 0.0 copy-start
  1.3 1.0 %copy-done = bf16[1024,256]{1,0:T(8,128)(2,1)S(1)} copy-done((bf16[1024,256]{1,0:T(8,128)(2,1)S(1)}, bf16[1024,256]{1,0:T(8,128)(2,1)}, u32[]{:S(2)}) %copy-start) | copy-done | bytes 524312
  2.3 0.0 copy-start.1
  2.3 1.0 %copy-done.1 = bf16[1024,256]{1,0:T(8,128)(2,1)S(1)} copy-done((bf16[1024,256]{1,0:T(8,128)(2,1)S(1)}, bf16[1024,256]{1,0:T(8,128)(2,1)}, u32[]{:S(2)}) %copy-start.1) | copy-done | bytes 524312
  3.4 71.8 %shard_map.58 = (bf16[1024,256]{1,0:T(8,128)(2,1)S(1)}, bf16[1024,256]{1,0:T(8,128)(2,1)S(1)}, f32[2,128]{1,0:T(2,128)S(1)}) custom-call(f32[1]{0:T(128)S(6)} %copy.9.factor_ref, bf16[1024,256]{1,0:T(8,128)(2,1)S(1)} %copy-done, bf16[1024,256]{1,0:T(8,128)(2,1)S(1)} %copy-done.1), custom_call_target="tpu_custom_call" | custom-call | flops 6442450944 | bytes 2097152 | tf_op jit(solution)/shard_map/pallas_call | solution.py:346
  75.2 0.8 %copy.10 = bf16[1024,256]{1,0:T(8,128)(2,1)} copy(bf16[1024,256]{1,0:T(8,128)(2,1)S(1)} %get-tuple-element.12) | data formatting | bytes 1048576
  76.0 0.8 %copy.11 = bf16[1024,256]{1,0:T(8,128)(2,1)} copy(bf16[1024,256]{1,0:T(8,128)(2,1)S(1)} %get-tuple-element.13) | data formatting | bytes 1048576
  76.7 0.6 copy.12
Async XLA Ops:
  1.3 1.0 %copy-start = (bf16[1024,256]{1,0:T(8,128)(2,1)S(1)}, bf16[1024,256]{1,0:T(8,128)(2,1)}, u32[]{:S(2)}) copy-start(bf16[1024,256]{1,0:T(8,128)(2,1)} %image_ref.1) | copy-start | bytes 1572868
  2.3 1.0 %copy-start.1 = (bf16[1024,256]{1,0:T(8,128)(2,1)S(1)}, bf16[1024,256]{1,0:T(8,128)(2,1)}, u32[]{:S(2)}) copy-start(bf16[1024,256]{1,0:T(8,128)(2,1)} %text_ref.1) | copy-start | bytes 1572868

commit v2 on v0

v2 whole, which is shorter than its diff:
```python
import functools

import jax
import jax.numpy as jnp
from jax import lax
from jax.experimental import pallas as pl
from jax.experimental.pallas import tpu as pltpu
from jax.sharding import PartitionSpec as P

MESH = pl.DeviceIdType.MESH
F32 = jnp.float32
BF16 = jnp.bfloat16
CHUNKS = 8
PAIRS = 4

Y_T = 0
Y_I = 4
C_I = 12
C_T = 13
C_V = 15
X_T = 19
X_V = 23
C_P = 27
C_F = 31
S_R = 39
S_N = 40
S_P = 41
V_X = 42
G_Y = 46
T_Y = 54
L_Y = 58
N_COPIES = 59


def dot_nt(a, b):
    return lax.dot_general(a, b, (((1,), (1,)), ((), ())), preferred_element_type=F32)


def dot_tn(a, b):
    return lax.dot_general(a, b, (((0,), (0,)), ((), ())), preferred_element_type=F32)


def dot_nn(a, b):
    return lax.dot_general(a, b, (((1,), (0,)), ((), ())), preferred_element_type=F32)


def log_add(a, b):
    top = jnp.maximum(a, b)
    return top + jnp.log(jnp.exp(a - top) + jnp.exp(b - top))


def kernel(
    n_dp,
    factor_ref,
    image_ref,
    text_ref,
    image_out,
    text_out,
    loss_out,
    full,
    text,
    score,
    row_part,
    col_max,
    col_sum,
    stat,
    row_lse,
    col_lse,
    prob,
    visit_out,
    visit_in,
    part_out,
    part_in,
    text_send,
    text_keep,
    image_keep,
    loss_own,
    loss_in,
    send_sem,
    recv_sem,
    local_sem,
):
    d = lax.axis_index("dp")
    m = lax.axis_index("mp")
    c_m = m + 1 - 2 * lax.rem(m, 2)
    y_m = lax.rem(m + 2, 4)
    nxt = lax.rem(d + 1, n_dp)
    prv = lax.rem(d + n_dp - 1, n_dp)
    half = n_dp // 2
    swap = lax.div(d, half)
    out_swap = lax.div(lax.rem(d, half) + 1, half)
    back_swap = 1 - lax.div(lax.rem(d, half) + half - 1, half)
    to_c, to_y = (d, c_m), (d, y_m)
    to_next = (nxt, lax.rem(m + 2 * out_swap, 4))
    to_prev = (prv, lax.rem(m + 2 * back_swap, 4))
    mine = lax.rem(m + 2 * swap, 4)
    other = lax.rem(c_m + 2 * swap, 4)
    mine_y = lax.rem(mine + 2, 4)
    other_y = lax.rem(other + 2, 4)

    def block(index, size=256):
        return pl.ds(pl.multiple_of(index * size, size), size)

    def remote(src, dst, index, device):
        return pltpu.make_async_remote_copy(
            src_ref=src,
            dst_ref=dst,
            send_sem=send_sem.at[index],
            recv_sem=recv_sem.at[index],
            device_id=device,
            device_id_type=MESH,
        )

    own, via = pl.ds(0, 256), pl.ds(256, 256)

    def piece(first, second, k):
        return block(2 * (first if k < 2 else second) + k % 2, 128)

    locals_ = [
        pltpu.make_async_copy(image_ref, full.at[:, own], local_sem.at[0]),
        pltpu.make_async_copy(text_ref.at[block(mine)], text.at[pl.ds(512, 256), own], local_sem.at[1]),
        pltpu.make_async_copy(text_ref.at[block(other)], text.at[pl.ds(768, 256), own], local_sem.at[2]),
    ]
    for copy in locals_:
        copy.start()

    barrier = pltpu.get_barrier_semaphore()
    for device in (to_c, to_y, to_prev):
        pl.semaphore_signal(barrier, inc=1, device_id=device, device_id_type=MESH)
    pl.semaphore_wait(barrier, 3)

    y_text = [
        remote(text_ref.at[piece(mine_y, other_y, k)], text.at[pl.ds(512 + 128 * k, 128), via], Y_T + k, to_y)
        for k in range(4)
    ]
    c_image = remote(image_ref, full.at[:, pl.ds(512, 256)], C_I, to_c)
    c_text = [
        remote(text_ref.at[block(other)], text.at[pl.ds(512, 256), pl.ds(512, 256)], C_T, to_c),
        remote(text_ref.at[block(mine)], text.at[pl.ds(768, 256), pl.ds(512, 256)], C_T + 1, to_c),
    ]
    c_via = [
        remote(
            text.at[pl.ds(512 + 128 * k, 128), via],
            text.at[pl.ds(512 + 128 * ((k + 2) % 4), 128), pl.ds(768, 256)],
            C_V + k,
            to_c,
        )
        for k in range(4)
    ]
    x_own = [
        remote(text_ref.at[piece(mine, other, k)], text.at[pl.ds(128 * k, 128), block(out_swap)], X_T + k, to_next)
        for k in range(4)
    ]
    x_via = [
        remote(
            text.at[pl.ds(512 + 128 * k, 128), via],
            text.at[pl.ds(128 * k, 128), block(1 - out_swap)],
            X_V + k,
            to_next,
        )
        for k in range(4)
    ]
    c_prev = [
        remote(
            text.at[pl.ds(128 * k, 128), pl.ds(0, 512)],
            text.at[pl.ds(128 * ((k + 2) % 4), 128), pl.ds(512, 512)],
            C_P + k,
            to_c,
        )
        for k in range(4)
    ]

    def y_image(r):
        return remote(image_ref.at[block(r, 128)], full.at[block(r, 128), via], Y_I + r, to_y)

    def c_forward(r):
        return remote(full.at[block(r, 128), via], full.at[block(r, 128), pl.ds(768, 256)], C_F + r, to_c)

    for k in range(4):
        y_text[k].start()
    for k in range(4):
        x_own[k].start()
    c_text[0].start()
    c_text[1].start()
    c_image.start()
    for r in range(CHUNKS):
        y_image(r).start()

    for k in range(4):
        y_text[k].wait_recv()
        x_via[k].start()
        c_via[k].start()
    for copy in locals_:
        copy.wait()
    for copy in [c_image] + c_text + c_via:
        copy.wait_recv()
    sent = y_text + [c_image] + c_text + c_via + x_own + x_via + c_prev

    factor = factor_ref[0]
    eye = lax.broadcasted_iota(jnp.int32, (128, 128), 0) == lax.broadcasted_iota(
        jnp.int32, (128, 128), 1
    )

    def arrive(p):
        for r in (2 * p, 2 * p + 1):
            y_image(r).wait_recv()
            c_forward(r).start()
        for r in (2 * p, 2 * p + 1):
            c_forward(r).wait_recv()

    def tile(t, p):
        scored = factor * dot_nt(text[512 * t : 512 * t + 512, :], full[block(p), :])
        score[p, 512 * t : 512 * t + 512, :] = scored
        top = jnp.max(scored, axis=0, keepdims=True)
        total = top + jnp.log(jnp.sum(jnp.exp(scored - top), axis=0, keepdims=True))
        for k in range(2):
            row_part[t, pl.ds(2 * p + k, 1), :] = total[:, 128 * k : 128 * k + 128]
        highest = jnp.max(scored, axis=1, keepdims=True)
        summed = jnp.sum(jnp.exp(scored - highest), axis=1, keepdims=True)
        for q in range(4):
            at = slice(128 * q, 128 * q + 128)
            col_max[p, 4 * t + q : 4 * t + q + 1, :] = jnp.sum(
                jnp.where(eye, highest[at], 0.0), axis=0, keepdims=True
            )
            col_sum[p, 4 * t + q : 4 * t + q + 1, :] = jnp.sum(
                jnp.where(eye, summed[at], 0.0), axis=0, keepdims=True
            )

    def own_chunk(p, carry):
        arrive(p)
        tile(1, p)
        return carry

    def prev_chunk(p, carry):
        tile(0, p)
        return carry

    def column(t):
        rows = slice(4 * t, 4 * t + 4)
        top = col_max[0, rows, :]
        for p in range(1, PAIRS):
            top = jnp.maximum(top, col_max[p, rows, :])
        total = jnp.zeros_like(top)
        for p in range(PAIRS):
            total = total + col_sum[p, rows, :] * jnp.exp(col_max[p, rows, :] - top)
        at = 2 - 2 * t
        stat[at, 0:4, :] = top + jnp.log(total)
        stat[at, 4:8, :] = jnp.zeros((4, 128), F32)

    to_n = remote(stat.at[0], stat.at[3], S_N, to_next)
    to_p = remote(stat.at[2], stat.at[1], S_P, to_prev)
    to_r = remote(stat.at[4], stat.at[5], S_R, to_y)

    first = lax.rem(d, half) == 0
    early = jnp.where(first, PAIRS, 2)
    later = jnp.where(first, PAIRS, 3)
    lax.fori_loop(0, early, own_chunk, 0)

    @pl.when(first)
    def _():
        column(1)
        to_n.start()

    for k in range(4):
        x_own[k].wait_recv()
        x_via[k].wait_recv()
        c_prev[k].start()
    for k in range(4):
        c_prev[k].wait_recv()
    lax.fori_loop(0, early, prev_chunk, 0)
    lax.fori_loop(early, later, own_chunk, 0)
    lax.fori_loop(early, later, prev_chunk, 0)
    lax.fori_loop(later, PAIRS, own_chunk, 0)

    @pl.when(jnp.logical_not(first))
    def _():
        column(1)
        to_n.start()

    lax.fori_loop(later, PAIRS, prev_chunk, 0)
    stat[4] = log_add(row_part[0], row_part[1])
    to_r.start()
    column(0)
    to_p.start()
    sent += [to_n, to_p, to_r]

    place = [2 * mine, 2 * mine + 1, 2 * other, 2 * other + 1]

    def diagonal_block(q):
        pair = mine if q < 2 else other
        return score[pair, 512 + 128 * q : 640 + 128 * q, 128 * (q % 2) : 128 * (q % 2) + 128]

    diagonal = [
        jnp.sum(
            jnp.where(eye, diagonal_block(q), 0.0), axis=0, keepdims=True
        )
        for q in range(4)
    ]

    def spread(lse, at):
        for q in range(4):
            col_lse[at + 128 * q : at + 128 * q + 128, :] = jnp.broadcast_to(
                lse[q : q + 1, :], (128, 128)
            ).T

    to_p.wait_recv()
    lse_own = log_add(stat[0, 0:4, :], stat[1, 0:4, :])
    spread(lse_own, 512)
    to_r.wait_recv()
    row_lse[...] = log_add(stat[4], stat[5])
    for q in range(4):
        loss_own[q : q + 1, :] = (
            0.5 * (row_lse[pl.ds(place[q], 1), :] + lse_own[q : q + 1, :]) - diagonal[q]
        )
    loss_own[4:8, :] = jnp.zeros((4, 128), F32)
    loss_copy = remote(loss_own, loss_in, L_Y, to_y)
    to_n.wait_recv()
    spread(log_add(stat[2, 0:4, :], stat[3, 0:4, :]), 0)

    def partial(r):
        return remote(part_out.at[block(r, 128)], part_in.at[block(r, 128)], G_Y + r, to_y)

    unit = eye.astype(F32)

    def probability(p, carry):
        for k in range(2):
            r = 2 * p + k
            lanes = block(r, 128)
            row = row_lse[pl.ds(r, 1), :]
            for q in range(8):
                at = slice(128 * q, 128 * q + 128)
                scored = score[p, at, 128 * k : 128 * k + 128]
                value = 0.5 * (jnp.exp(scored - row) + jnp.exp(scored - col_lse[at, :]))
                if q >= 4:
                    value = value - jnp.where(r == place[q - 4], unit, 0.0)
                prob[at, lanes] = value.astype(BF16)
            part_out[lanes, :] = dot_tn(prob[:, lanes], text[:, 256:512]).astype(BF16)
            partial(r).start()
        return carry

    lax.fori_loop(0, PAIRS, probability, 0)
    loss_copy.start()

    def visit(k):
        rows = pl.ds(256 * (k % 2), 256)
        kept = 1 - k // 2
        taken = lax.rem(kept + back_swap, 2)
        return remote(
            visit_out.at[rows, block(taken)], visit_in.at[rows, pl.ds(256 * kept, 256)], V_X + k, to_prev
        )

    for kept in (1, 0):
        lanes = block(lax.rem(kept + back_swap, 2))
        for rows in (slice(0, 256), slice(256, 512)):
            visit_out[rows, lanes] = dot_nn(prob[rows, :], full[:, lanes]).astype(BF16)
        visit(2 * (1 - kept)).start()
        visit(2 * (1 - kept) + 1).start()

    image_copies = [
        pltpu.make_async_copy(
            image_keep.at[pl.ds(512 * k, 512)], image_out.at[pl.ds(512 * k, 512)], local_sem.at[3 + k]
        )
        for k in range(2)
    ]

    def image_final(r, carry):
        lanes = block(r, 128)
        value = dot_tn(prob[:, lanes], text[:, 0:256])
        partial(r).wait_recv()
        image_keep[lanes, :] = (factor * (value + part_in[lanes, :].astype(F32))).astype(BF16)
        return carry

    def text_value(k):
        rows = slice(256 * (k % 2), 256 * (k % 2) + 256)
        lanes = slice(256, 512) if k < 2 else slice(0, 256)
        own_term = dot_nn(prob[512 + rows.start : 512 + rows.stop, :], full[:, lanes])
        visit(k).wait_recv()
        return (factor * (own_term + visit_in[rows, lanes].astype(F32))).astype(BF16)

    text_copies = []
    for k in range(2):
        rows = pl.ds(256 * k, 256)
        target = text_out.at[block(mine if k == 0 else other)]
        text_copies.append(remote(text_send.at[rows], target, T_Y + k, to_y))
    keep_copies = [
        pltpu.make_async_copy(
            text_keep.at[pl.ds(256 * k, 256)],
            text_out.at[block(mine if k == 0 else other)],
            local_sem.at[5 + k],
        )
        for k in range(2)
    ]

    lax.fori_loop(0, 4, image_final, 0)
    image_copies[0].start()
    for k in range(2):
        text_send[256 * k : 256 * k + 256, :] = text_value(k)
        text_copies[k].start()
    lax.fori_loop(4, CHUNKS, image_final, 0)
    image_copies[1].start()
    for k in range(2):
        text_keep[256 * k : 256 * k + 256, :] = text_value(2 + k)
        keep_copies[k].start()

    loss_copy.wait_recv()
    loss_out[...] = jnp.where(swap == 1, loss_in[0:2, :], loss_own[0:2, :])
    for copy in sent + [loss_copy] + text_copies:
        copy.wait_send()
    for k in range(4):
        visit(k).wait_send()
    for r in range(CHUNKS):
        y_image(r).wait_send()
        c_forward(r).wait_send()
        partial(r).wait_send()
    for copy in image_copies + keep_copies:
        copy.wait()
    for copy in text_copies:
        copy.wait_recv()


def local(n_dp, image_emb, text_emb, logit_scale):
    vmem = pltpu.VMEM
    image_grad, text_grad, loss = pl.pallas_call(
        functools.partial(kernel, n_dp),
        out_shape=(
            jax.ShapeDtypeStruct((1024, 256), BF16),
            jax.ShapeDtypeStruct((1024, 256), BF16),
            jax.ShapeDtypeStruct((2, 128), F32),
        ),
        in_specs=[
            pl.BlockSpec(memory_space=pltpu.SMEM),
            pl.BlockSpec(memory_space=pl.ANY),
            pl.BlockSpec(memory_space=pl.ANY),
        ],
        out_specs=[
            pl.BlockSpec(memory_space=pl.ANY),
            pl.BlockSpec(memory_space=pl.ANY),
            pl.BlockSpec(memory_space=vmem),
        ],
        scratch_shapes=[
            vmem((1024, 1024), BF16),
            vmem((1024, 1024), BF16),
            vmem((PAIRS, 1024, 256), F32),
            vmem((2, 8, 128), F32),
            vmem((PAIRS, 8, 128), F32),
            vmem((PAIRS, 8, 128), F32),
            vmem((6, 8, 128), F32),
            vmem((8, 128), F32),
            vmem((1024, 128), F32),
            vmem((1024, 1024), BF16),
            vmem((512, 512), BF16),
            vmem((512, 512), BF16),
            vmem((1024, 256), BF16),
            vmem((1024, 256), BF16),
            vmem((512, 256), BF16),
            vmem((512, 256), BF16),
            vmem((1024, 256), BF16),
            vmem((8, 128), F32),
            vmem((8, 128), F32),
            pltpu.SemaphoreType.DMA((N_COPIES,)),
            pltpu.SemaphoreType.DMA((N_COPIES,)),
            pltpu.SemaphoreType.DMA((7,)),
        ],
        compiler_params=pltpu.CompilerParams(
            collective_id=0, has_side_effects=True, vmem_limit_bytes=60 * 1024 * 1024
        ),
        cost_estimate=pl.CostEstimate(
            flops=4 * 2**31, bytes_accessed=2**21, transcendentals=2**22
        ),
    )(logit_scale, image_emb, text_emb)
    return image_grad, text_grad, loss.reshape(256)


def solution(mesh):
    return jax.shard_map(
        functools.partial(local, mesh.shape["dp"]),
        mesh=mesh,
        in_specs=(P("dp", "mp"), P("dp", "mp"), P()),
        out_specs=(P("dp", "mp"), P("dp", "mp"), P(("dp", "mp"))),
        check_vma=False,
    )
```

time: 261 us -> 60.2 us (0.23)
  waiting for transfers between devices: 202 us -> 0 us
  Pallas kernels: 0 us -> 55.5 us
  matrix products: 14.9 us -> 0 us
  between operations: 14.8 us -> 1.3 us
  other arithmetic: 13 us -> 0 us
  starting transfers between devices: 11.9 us -> 0 us
    psum x1 -> x0, waiting for transfers between devices: 158 us -> none  [local(): lax.psum((contract_width(image_emb, text_emb), contract_width(image_emb,...]
    pallas_call x0 -> x1, Pallas kernels: none -> 55.5 us  [local(): pl.pallas_call(functools.partial(kernel, n_dp), out_shape=(jax.ShapeDtype...]
    ppermute x4 -> x0, waiting for transfers between devices: 43.8 us -> none  [the longest x2 33.7 us: shifted(): lax.ppermute(x, axis, [(i, (i + by) % devices) for i in range(devices)])]
    dot_general x6 -> x0, matrix products: 14.9 us -> none  [the longest x2 6.49 us: contract_width(): lax.dot_general(left_rows, right_rows, (((1,), (1,)), ((), ())), preferre...]
    ppermute x4 -> x0, starting transfers between devices: 11.8 us -> none  [the longest x1 8.15 us: with_halo(): lax.ppermute(head, axis, [((i + 1) % count, i) for i in range(count)])]
    reduce_sum x3 -> x0, other arithmetic: 4.83 us -> none  [the longest x1 3.37 us: local(): diagonal = jnp.sum(score_own * identity, axis=1)]
    reduce_max x1 -> x0, other arithmetic: 4.22 us -> none  [row_logsumexp(): jnp.max(score_prev, axis=1)]
    convert_element_type x1 -> x0, other arithmetic: 3.81 us -> none  [local(): prob_prev = (0.5 * (jnp.exp(score_prev - row_lse[:, None]) + jnp.exp(scor...]
  transfers between devices with their start and end apart: 5 -> 0, of which waited for: 5 -> 0; matrix products, arithmetic and copies ran while one was open for 3% -> 0% of each run, Pallas kernels for 0% -> 0%
where the time goes in v2:
time: 60.2 us; the launch traced here: 60.1 us
  Pallas kernels  55.5 us (92%)
  local copies, waits for them, and re-layouts  3.29 us (5%)
  between operations  1.3 us (2%)
    pallas_call x1, Pallas kernels, local(): pl.pallas_call(functools.partial(kernel, n_dp), out_shape=(jax.ShapeDtype...  55.5 us
    unnamed x7, local copies, waits for them, and re-layouts  3.29 us

profile of v2, /device:TPU:8, one launch (start us, length us, event | category | flops | bytes accessed | tf_op | source)
XLA Modules:
  0.0 60.1 jit_solution(2080460548009980400)
XLA Ops:
  1.3 55.5 %shard_map.58 = (bf16[1024,256]{1,0:T(8,128)(2,1)}, bf16[1024,256]{1,0:T(8,128)(2,1)}, f32[2,128]{1,0:T(2,128)}) custom-call(f32[1]{0:T(128)S(6)} %copy.9.factor_ref, bf16[1024,256]{1,0:T(8,128)(2,1)} %image_ref.1, bf16[1024,256]{1,0:T(8,128)(2,1)} %text_ref.1), custom_call_target="tpu_custom_call" | custom-call | flops 8589934592 | bytes 2097152 | tf_op jit(solution)/shard_map/pallas_call | solution.py:423
  56.8 0.0 copy-start
  56.8 1.9 %copy.10 = bf16[1024,256]{1,0:T(8,128)(2,1)} copy(bf16[1024,256]{1,0:T(8,128)(2,1)} %get-tuple-element.12) | data formatting | bytes 1048576
  58.7 0.0 copy-done
  58.7 0.0 copy-start.1
  58.7 0.8 %copy.11 = bf16[1024,256]{1,0:T(8,128)(2,1)} copy(bf16[1024,256]{1,0:T(8,128)(2,1)S(1)} %copy-done) | data formatting | bytes 1048576
  59.5 0.0 copy-done.1
  59.5 0.6 copy.12
Async XLA Ops:
  56.8 1.9 %copy-start = (bf16[1024,256]{1,0:T(8,128)(2,1)S(1)}, bf16[1024,256]{1,0:T(8,128)(2,1)}, u32[]{:S(2)}) copy-start(bf16[1024,256]{1,0:T(8,128)(2,1)} %get-tuple-element.13) | copy-start | bytes 1572868
  58.7 0.8 %copy-start.1 = (f32[2,128]{1,0:T(2,128)S(1)}, f32[2,128]{1,0:T(2,128)}, u32[]{:S(2)}) copy-start(f32[2,128]{1,0:T(2,128)} %get-tuple-element.8) | copy-start | bytes 3076

commit v3 on v2

--- a/solution.py
+++ b/solution.py
@@ -72,8 +72,6 @@
     part_out,
     part_in,
     text_send,
-    text_keep,
-    image_keep,
     loss_own,
     loss_in,
     send_sem,
@@ -251,33 +249,16 @@
     to_p = remote(stat.at[2], stat.at[1], S_P, to_prev)
     to_r = remote(stat.at[4], stat.at[5], S_R, to_y)
 
-    first = lax.rem(d, half) == 0
-    early = jnp.where(first, PAIRS, 2)
-    later = jnp.where(first, PAIRS, 3)
-    lax.fori_loop(0, early, own_chunk, 0)
-
-    @pl.when(first)
-    def _():
-        column(1)
-        to_n.start()
-
+    lax.fori_loop(0, PAIRS, own_chunk, 0)
+    column(1)
+    to_n.start()
     for k in range(4):
         x_own[k].wait_recv()
         x_via[k].wait_recv()
         c_prev[k].start()
     for k in range(4):
         c_prev[k].wait_recv()
-    lax.fori_loop(0, early, prev_chunk, 0)
-    lax.fori_loop(early, later, own_chunk, 0)
-    lax.fori_loop(early, later, prev_chunk, 0)
-    lax.fori_loop(later, PAIRS, own_chunk, 0)
-
-    @pl.when(jnp.logical_not(first))
-    def _():
-        column(1)
-        to_n.start()
-
-    lax.fori_loop(later, PAIRS, prev_chunk, 0)
+    lax.fori_loop(0, PAIRS, prev_chunk, 0)
     stat[4] = log_add(row_part[0], row_part[1])
     to_r.start()
     column(0)
@@ -314,31 +295,41 @@
         )
     loss_own[4:8, :] = jnp.zeros((4, 128), F32)
     loss_copy = remote(loss_own, loss_in, L_Y, to_y)
+    unit = eye.astype(F32)
+
+    def probability(p, k, q):
+        at = slice(128 * q, 128 * q + 128)
+        r = 2 * p + k
+        scored = score[p, at, 128 * k : 128 * k + 128]
+        row = row_lse[pl.ds(r, 1), :]
+        value = 0.5 * (jnp.exp(scored - row) + jnp.exp(scored - col_lse[at, :]))
+        if q >= 4:
+            value = value - jnp.where(r == place[q - 4], unit, 0.0)
+        prob[at, block(r, 128)] = value.astype(BF16)
+
+    def own_probability(p, carry):
+        for k in range(2):
+            for q in range(4, 8):
+                probability(p, k, q)
+        return carry
+
+    lax.fori_loop(0, PAIRS, own_probability, 0)
     to_n.wait_recv()
     spread(log_add(stat[2, 0:4, :], stat[3, 0:4, :]), 0)
 
     def partial(r):
         return remote(part_out.at[block(r, 128)], part_in.at[block(r, 128)], G_Y + r, to_y)
 
-    unit = eye.astype(F32)
-
-    def probability(p, carry):
+    def prev_probability(p, carry):
         for k in range(2):
-            r = 2 * p + k
-            lanes = block(r, 128)
-            row = row_lse[pl.ds(r, 1), :]
-            for q in range(8):
-                at = slice(128 * q, 128 * q + 128)
-                scored = score[p, at, 128 * k : 128 * k + 128]
-                value = 0.5 * (jnp.exp(scored - row) + jnp.exp(scored - col_lse[at, :]))
-                if q >= 4:
-                    value = value - jnp.where(r == place[q - 4], unit, 0.0)
-                prob[at, lanes] = value.astype(BF16)
+            for q in range(4):
+                probability(p, k, q)
+            lanes = block(2 * p + k, 128)
             part_out[lanes, :] = dot_tn(prob[:, lanes], text[:, 256:512]).astype(BF16)
-            partial(r).start()
+            partial(2 * p + k).start()
         return carry
 
-    lax.fori_loop(0, PAIRS, probability, 0)
+    lax.fori_loop(0, PAIRS, prev_probability, 0)
     loss_copy.start()
 
     def visit(k):
@@ -356,18 +347,11 @@
         visit(2 * (1 - kept)).start()
         visit(2 * (1 - kept) + 1).start()
 
-    image_copies = [
-        pltpu.make_async_copy(
-            image_keep.at[pl.ds(512 * k, 512)], image_out.at[pl.ds(512 * k, 512)], local_sem.at[3 + k]
-        )
-        for k in range(2)
-    ]
-
     def image_final(r, carry):
         lanes = block(r, 128)
         value = dot_tn(prob[:, lanes], text[:, 0:256])
         partial(r).wait_recv()
-        image_keep[lanes, :] = (factor * (value + part_in[lanes, :].astype(F32))).astype(BF16)
+        image_out[lanes, :] = (factor * (value + part_in[lanes, :].astype(F32))).astype(BF16)
         return carry
 
     def text_value(k):
@@ -382,25 +366,13 @@
         rows = pl.ds(256 * k, 256)
         target = text_out.at[block(mine if k == 0 else other)]
         text_copies.append(remote(text_send.at[rows], target, T_Y + k, to_y))
-    keep_copies = [
-        pltpu.make_async_copy(
-            text_keep.at[pl.ds(256 * k, 256)],
-            text_out.at[block(mine if k == 0 else other)],
-            local_sem.at[5 + k],
-        )
-        for k in range(2)
-    ]
-
     lax.fori_loop(0, 4, image_final, 0)
-    image_copies[0].start()
     for k in range(2):
         text_send[256 * k : 256 * k + 256, :] = text_value(k)
         text_copies[k].start()
     lax.fori_loop(4, CHUNKS, image_final, 0)
-    image_copies[1].start()
     for k in range(2):
-        text_keep[256 * k : 256 * k + 256, :] = text_value(2 + k)
-        keep_copies[k].start()
+        text_out[block(mine if k == 0 else other), :] = text_value(2 + k)
 
     loss_copy.wait_recv()
     loss_out[...] = jnp.where(swap == 1, loss_in[0:2, :], loss_own[0:2, :])
@@ -412,10 +384,21 @@
         y_image(r).wait_send()
         c_forward(r).wait_send()
         partial(r).wait_send()
-    for copy in image_copies + keep_copies:
-        copy.wait()
     for copy in text_copies:
         copy.wait_recv()
+
+
+def finish(image_ref, text_ref, loss_ref, image_out, text_out, loss_out, sem):
+    copies = [
+        pltpu.make_async_copy(image_ref, image_out, sem.at[0]),
+        pltpu.make_async_copy(text_ref, text_out, sem.at[1]),
+    ]
+    for copy in copies:
+        copy.start()
+    for k in range(2):
+        loss_out[pl.ds(128 * k, 128)] = loss_ref[k, :]
+    for copy in copies:
+        copy.wait()
 
 
 def local(n_dp, image_emb, text_emb, logit_scale):
@@ -423,20 +406,16 @@
     image_grad, text_grad, loss = pl.pallas_call(
         functools.partial(kernel, n_dp),
         out_shape=(
-            jax.ShapeDtypeStruct((1024, 256), BF16),
-            jax.ShapeDtypeStruct((1024, 256), BF16),
-            jax.ShapeDtypeStruct((2, 128), F32),
+            vmem((1024, 256), BF16),
+            vmem((1024, 256), BF16),
+            vmem((2, 128), F32),
         ),
         in_specs=[
             pl.BlockSpec(memory_space=pltpu.SMEM),
             pl.BlockSpec(memory_space=pl.ANY),
             pl.BlockSpec(memory_space=pl.ANY),
         ],
-        out_specs=[
-            pl.BlockSpec(memory_space=pl.ANY),
-            pl.BlockSpec(memory_space=pl.ANY),
-            pl.BlockSpec(memory_space=vmem),
-        ],
+        out_specs=[pl.BlockSpec(memory_space=vmem)] * 3,
         scratch_shapes=[
             vmem((1024, 1024), BF16),
             vmem((1024, 1024), BF16),
@@ -453,22 +432,34 @@
             vmem((1024, 256), BF16),
             vmem((1024, 256), BF16),
             vmem((512, 256), BF16),
-            vmem((512, 256), BF16),
-            vmem((1024, 256), BF16),
             vmem((8, 128), F32),
             vmem((8, 128), F32),
             pltpu.SemaphoreType.DMA((N_COPIES,)),
             pltpu.SemaphoreType.DMA((N_COPIES,)),
-            pltpu.SemaphoreType.DMA((7,)),
+            pltpu.SemaphoreType.DMA((3,)),
         ],
         compiler_params=pltpu.CompilerParams(
-            collective_id=0, has_side_effects=True, vmem_limit_bytes=60 * 1024 * 1024
+            collective_id=0, has_side_effects=True, vmem_limit_bytes=56 * 1024 * 1024
         ),
         cost_estimate=pl.CostEstimate(
             flops=4 * 2**31, bytes_accessed=2**21, transcendentals=2**22
         ),
     )(logit_scale, image_emb, text_emb)
-    return image_grad, text_grad, loss.reshape(256)
+    return pl.pallas_call(
+        finish,
+        out_shape=(
+            jax.ShapeDtypeStruct((1024, 256), BF16),
+            jax.ShapeDtypeStruct((1024, 256), BF16),
+            jax.ShapeDtypeStruct((256,), F32),
+        ),
+        in_specs=[pl.BlockSpec(memory_space=vmem)] * 3,
+        out_specs=[
+            pl.BlockSpec(memory_space=pl.ANY),
+            pl.BlockSpec(memory_space=pl.ANY),
+            pl.BlockSpec(memory_space=vmem),
+        ],
+        scratch_shapes=[pltpu.SemaphoreType.DMA((2,))],
+    )(*(pltpu.with_memory_space_constraint(x, vmem) for x in (image_grad, text_grad, loss)))
 
 
 def solution(mesh):

time: 60.2 us -> 55.7 us (0.925)
  local copies, waits for them, and re-layouts: 3.29 us -> 0 us
  Pallas kernels: 55.5 us -> 54.3 us
    unnamed x7 -> x0, local copies, waits for them, and re-layouts: 3.29 us -> none
    pallas_call x1 -> x2, Pallas kernels: 55.5 us -> 54.3 us  [the longest x1 52.8 us: local(): pl.pallas_call(functools.partial(kernel, n_dp), out_shape=(vmem((1024, 25...]
where the time goes in v3:
time: 55.7 us; the launch traced here: 55.6 us
  Pallas kernels  54.3 us (97%)
  between operations  1.28 us (2%)
    pallas_call x1, Pallas kernels, local(): pl.pallas_call(functools.partial(kernel, n_dp), out_shape=(vmem((1024, 25...  52.8 us
    pallas_call x1, Pallas kernels, local(): pl.pallas_call(finish, out_shape=(jax.ShapeDtypeStruct((1024, 256), BF16)...  1.55 us

profile of v3, /device:TPU:8, one launch (start us, length us, event | category | flops | bytes accessed | tf_op | source)
XLA Modules:
  0.0 55.6 jit_solution(5508141872055746466)
XLA Ops:
  1.3 52.8 %shard_map.58 = (bf16[1024,256]{1,0:T(8,128)(2,1)S(1)}, bf16[1024,256]{1,0:T(8,128)(2,1)S(1)}, f32[2,128]{1,0:T(2,128)S(1)}) custom-call(f32[1]{0:T(128)S(6)} %copy.6.factor_ref, bf16[1024,256]{1,0:T(8,128)(2,1)} %image_ref.1, bf16[1024,256]{1,0:T(8,128)(2,1)} %text_ref.1), custom_call_target="tpu_custom_call" | custom-call | flops 8589934592 | bytes 2097152 | tf_op jit(solution)/shard_map/pallas_call | solution.py:406
  54.0 1.5 %shard_map.59 = (bf16[1024,256]{1,0:T(8,128)(2,1)}, bf16[1024,256]{1,0:T(8,128)(2,1)}, f32[256]{0:T(256)}) custom-call(bf16[1024,256]{1,0:T(8,128)(2,1)S(1)} %get-tuple-element.6.image_ref, bf16[1024,256]{1,0:T(8,128)(2,1)S(1)} %get-tuple-element.7.text_ref, f32[2,128]{1,0:T(2,128)S(1)} %get-tuple-element.8.loss_ref), custom_call_target="tpu_custom_call" | custom-call | tf_op jit(solution)/shard_map/pallas_call | solution.py:448

commit v4 on v3

--- a/solution.py
+++ b/solution.py
@@ -29,7 +29,9 @@
 G_Y = 46
 T_Y = 54
 L_Y = 58
-N_COPIES = 59
+R_A = 59
+R_B = 60
+N_COPIES = 61
 
 
 def dot_nt(a, b):
@@ -74,6 +76,8 @@
     text_send,
     loss_own,
     loss_in,
+    relay_a,
+    relay_b,
     send_sem,
     recv_sem,
     local_sem,
@@ -91,6 +95,11 @@
     to_c, to_y = (d, c_m), (d, y_m)
     to_next = (nxt, lax.rem(m + 2 * out_swap, 4))
     to_prev = (prv, lax.rem(m + 2 * back_swap, 4))
+    place_in_half = lax.rem(d, half)
+    first = place_in_half == 0
+    relay = (place_in_half == 1) | (place_in_half == 4)
+    base = d - place_in_half
+    last = place_in_half == half - 1
     mine = lax.rem(m + 2 * swap, 4)
     other = lax.rem(c_m + 2 * swap, 4)
     mine_y = lax.rem(mine + 2, 4)
@@ -99,12 +108,12 @@
     def block(index, size=256):
         return pl.ds(pl.multiple_of(index * size, size), size)
 
-    def remote(src, dst, index, device):
+    def remote(src, dst, index, device, arrival=None):
         return pltpu.make_async_remote_copy(
             src_ref=src,
             dst_ref=dst,
             send_sem=send_sem.at[index],
-            recv_sem=recv_sem.at[index],
+            recv_sem=recv_sem.at[index if arrival is None else arrival],
             device_id=device,
             device_id_type=MESH,
         )
@@ -119,13 +128,25 @@
         pltpu.make_async_copy(text_ref.at[block(mine)], text.at[pl.ds(512, 256), own], local_sem.at[1]),
         pltpu.make_async_copy(text_ref.at[block(other)], text.at[pl.ds(768, 256), own], local_sem.at[2]),
     ]
-    for copy in locals_:
-        copy.start()
-
     barrier = pltpu.get_barrier_semaphore()
     for device in (to_c, to_y, to_prev):
         pl.semaphore_signal(barrier, inc=1, device_id=device, device_id_type=MESH)
-    pl.semaphore_wait(barrier, 3)
+
+    @pl.when(place_in_half == 4)
+    def _():
+        pl.semaphore_signal(barrier, inc=1, device_id=(base, m), device_id_type=MESH)
+
+    for copy in locals_:
+        copy.start()
+
+    @pl.when(first)
+    def _():
+        pl.semaphore_wait(barrier, 4)
+
+    @pl.when(jnp.logical_not(first))
+    def _():
+        pl.semaphore_wait(barrier, 3)
+
 
     y_text = [
         remote(text_ref.at[piece(mine_y, other_y, k)], text.at[pl.ds(512 + 128 * k, 128), via], Y_T + k, to_y)
@@ -249,16 +270,32 @@
     to_p = remote(stat.at[2], stat.at[1], S_P, to_prev)
     to_r = remote(stat.at[4], stat.at[5], S_R, to_y)
 
-    lax.fori_loop(0, PAIRS, own_chunk, 0)
-    column(1)
-    to_n.start()
+    early = jnp.where(first | last, PAIRS, 2)
+    later = jnp.where(first | last, PAIRS, 3)
+    lax.fori_loop(0, early, own_chunk, 0)
+
+    @pl.when(first | last)
+    def _():
+        column(1)
+        to_n.start()
+
     for k in range(4):
         x_own[k].wait_recv()
         x_via[k].wait_recv()
         c_prev[k].start()
     for k in range(4):
         c_prev[k].wait_recv()
-    lax.fori_loop(0, PAIRS, prev_chunk, 0)
+    lax.fori_loop(0, early, prev_chunk, 0)
+    lax.fori_loop(early, later, own_chunk, 0)
+    lax.fori_loop(early, later, prev_chunk, 0)
+    lax.fori_loop(later, PAIRS, own_chunk, 0)
+
+    @pl.when(jnp.logical_not(first | last))
+    def _():
+        column(1)
+        to_n.start()
+
+    lax.fori_loop(later, PAIRS, prev_chunk, 0)
     stat[4] = log_add(row_part[0], row_part[1])
     to_r.start()
     column(0)
@@ -313,20 +350,48 @@
                 probability(p, k, q)
         return carry
 
-    lax.fori_loop(0, PAIRS, own_probability, 0)
+    lax.fori_loop(0, jnp.where(first, PAIRS, 0), own_probability, 0)
     to_n.wait_recv()
     spread(log_add(stat[2, 0:4, :], stat[3, 0:4, :]), 0)
 
     def partial(r):
         return remote(part_out.at[block(r, 128)], part_in.at[block(r, 128)], G_Y + r, to_y)
 
+    def relay_out(p):
+        r = 2 * p + 1
+        return remote(part_out.at[block(r, 128)], relay_a, G_Y + r, (base + 4 - 3 * p, m), R_A)
+
+    passed = jnp.where(place_in_half == 1, 3, 1)
+    relay_in = remote(relay_a, relay_a, R_A, to_y)
+    relay_over = remote(relay_a, relay_b, R_B, to_y)
+    relay_back = remote(relay_b, part_in.at[block(passed, 128)], R_A, (base, m), G_Y + passed)
+
     def prev_probability(p, carry):
+        @pl.when(jnp.logical_not(first))
+        def _():
+            own_probability(p, 0)
+
         for k in range(2):
             for q in range(4):
                 probability(p, k, q)
             lanes = block(2 * p + k, 128)
             part_out[lanes, :] = dot_tn(prob[:, lanes], text[:, 256:512]).astype(BF16)
-            partial(2 * p + k).start()
+            if k == 0:
+
+                @pl.when(jnp.logical_not(relay & (p == 3)))
+                def _():
+                    partial(2 * p).start()
+
+            else:
+
+                @pl.when(first & (p < 2))
+                def _():
+                    relay_out(p).start()
+
+                @pl.when(jnp.logical_not(first & (p < 2) | relay & (p == 3)))
+                def _():
+                    partial(2 * p + 1).start()
+
         return carry
 
     lax.fori_loop(0, PAIRS, prev_probability, 0)
@@ -340,14 +405,32 @@
             visit_out.at[rows, block(taken)], visit_in.at[rows, pl.ds(256 * kept, 256)], V_X + k, to_prev
         )
 
-    for kept in (1, 0):
+    def visiting(kept):
         lanes = block(lax.rem(kept + back_swap, 2))
         for rows in (slice(0, 256), slice(256, 512)):
             visit_out[rows, lanes] = dot_nn(prob[rows, :], full[:, lanes]).astype(BF16)
-        visit(2 * (1 - kept)).start()
-        visit(2 * (1 - kept) + 1).start()
-
-    def image_final(r, carry):
+
+    visiting(1)
+    visit(0).start()
+    visit(1).start()
+
+    @pl.when(relay)
+    def _():
+        relay_in.wait_recv()
+        relay_over.start()
+        partial(6).start()
+        partial(7).start()
+
+    visiting(0)
+
+    @pl.when(jnp.logical_not(relay))
+    def _():
+        visit(2).start()
+        visit(3).start()
+
+    def image_final(i, carry):
+        late = jnp.where(i < 2, 2 * i, jnp.where(i < 6, i + 2, 2 * i - 11))
+        r = jnp.where(first, late, i)
         lanes = block(r, 128)
         value = dot_tn(prob[:, lanes], text[:, 0:256])
         partial(r).wait_recv()
@@ -370,6 +453,14 @@
     for k in range(2):
         text_send[256 * k : 256 * k + 256, :] = text_value(k)
         text_copies[k].start()
+
+    @pl.when(relay)
+    def _():
+        relay_over.wait_recv()
+        relay_back.start()
+        visit(2).start()
+        visit(3).start()
+
     lax.fori_loop(4, CHUNKS, image_final, 0)
     for k in range(2):
         text_out[block(mine if k == 0 else other), :] = text_value(2 + k)
@@ -378,6 +469,12 @@
     loss_out[...] = jnp.where(swap == 1, loss_in[0:2, :], loss_own[0:2, :])
     for copy in sent + [loss_copy] + text_copies:
         copy.wait_send()
+
+    @pl.when(relay)
+    def _():
+        relay_over.wait_send()
+        relay_back.wait_send()
+
     for k in range(4):
         visit(k).wait_send()
     for r in range(CHUNKS):
@@ -389,10 +486,11 @@
 
 
 def finish(image_ref, text_ref, loss_ref, image_out, text_out, loss_out, sem):
-    copies = [
-        pltpu.make_async_copy(image_ref, image_out, sem.at[0]),
-        pltpu.make_async_copy(text_ref, text_out, sem.at[1]),
-    ]
+    copies = []
+    for k in range(4):
+        rows = pl.ds(256 * k, 256)
+        copies.append(pltpu.make_async_copy(image_ref.at[rows], image_out.at[rows], sem.at[k]))
+        copies.append(pltpu.make_async_copy(text_ref.at[rows], text_out.at[rows], sem.at[4 + k]))
     for copy in copies:
         copy.start()
     for k in range(2):
@@ -434,6 +532,8 @@
             vmem((512, 256), BF16),
             vmem((8, 128), F32),
             vmem((8, 128), F32),
+            vmem((128, 256), BF16),
+            vmem((128, 256), BF16),
             pltpu.SemaphoreType.DMA((N_COPIES,)),
             pltpu.SemaphoreType.DMA((N_COPIES,)),
             pltpu.SemaphoreType.DMA((3,)),
@@ -458,7 +558,7 @@
             pl.BlockSpec(memory_space=pl.ANY),
             pl.BlockSpec(memory_space=vmem),
         ],
-        scratch_shapes=[pltpu.SemaphoreType.DMA((2,))],
+        scratch_shapes=[pltpu.SemaphoreType.DMA((8,))],
     )(*(pltpu.with_memory_space_constraint(x, vmem) for x in (image_grad, text_grad, loss)))
 
 

time: 55.7 us -> 54.4 us (0.977)
  the two profiles are of different devices: /device:TPU:8 before, /device:TPU:6 now
where the time goes in v4:
time: 54.4 us; the launch traced here: 54.3 us
  Pallas kernels  53.1 us (98%)
  between operations  1.28 us (2%)
    pallas_call x1, Pallas kernels, local(): pl.pallas_call(functools.partial(kernel, n_dp), out_shape=(vmem((1024, 25...  51.5 us
    pallas_call x1, Pallas kernels, local(): pl.pallas_call(finish, out_shape=(jax.ShapeDtypeStruct((1024, 256), BF16)...  1.59 us

profile of v4, /device:TPU:6, one launch (start us, length us, event | category | flops | bytes accessed | tf_op | source)
XLA Modules:
  0.0 54.3 jit_solution(14910192121266097231)
XLA Ops:
  1.3 51.5 %shard_map.58 = (bf16[1024,256]{1,0:T(8,128)(2,1)S(1)}, bf16[1024,256]{1,0:T(8,128)(2,1)S(1)}, f32[2,128]{1,0:T(2,128)S(1)}) custom-call(f32[1]{0:T(128)S(6)} %copy.6.factor_ref, bf16[1024,256]{1,0:T(8,128)(2,1)} %image_ref.1, bf16[1024,256]{1,0:T(8,128)(2,1)} %text_ref.1), custom_call_target="tpu_custom_call" | custom-call | flops 8589934592 | bytes 2097152 | tf_op jit(solution)/shard_map/pallas_call | solution.py:504
  52.8 1.6 %shard_map.59 = (bf16[1024,256]{1,0:T(8,128)(2,1)}, bf16[1024,256]{1,0:T(8,128)(2,1)}, f32[256]{0:T(256)}) custom-call(bf16[1024,256]{1,0:T(8,128)(2,1)S(1)} %get-tuple-element.6.image_ref, bf16[1024,256]{1,0:T(8,128)(2,1)S(1)} %get-tuple-element.7.text_ref, f32[2,128]{1,0:T(2,128)S(1)} %get-tuple-element.8.loss_ref), custom_call_target="tpu_custom_call" | custom-call | tf_op jit(solution)/shard_map/pallas_call | solution.py:548

commit v5 on v4

--- a/solution.py
+++ b/solution.py
@@ -220,15 +220,16 @@
         jnp.int32, (128, 128), 1
     )
 
-    def arrive(p):
+    def arrive(p, rows):
         for r in (2 * p, 2 * p + 1):
             y_image(r).wait_recv()
             c_forward(r).start()
+        scored = dot_nt(text[rows, 0:768], full[block(p), 0:768])
         for r in (2 * p, 2 * p + 1):
             c_forward(r).wait_recv()
-
-    def tile(t, p):
-        scored = factor * dot_nt(text[512 * t : 512 * t + 512, :], full[block(p), :])
+        return factor * (scored + dot_nt(text[rows, 768:1024], full[block(p), 768:1024]))
+
+    def statistics(t, p, scored):
         score[p, 512 * t : 512 * t + 512, :] = scored
         top = jnp.max(scored, axis=0, keepdims=True)
         total = top + jnp.log(jnp.sum(jnp.exp(scored - top), axis=0, keepdims=True))
@@ -246,12 +247,11 @@
             )
 
     def own_chunk(p, carry):
-        arrive(p)
-        tile(1, p)
+        statistics(1, p, arrive(p, slice(512, 1024)))
         return carry
 
     def prev_chunk(p, carry):
-        tile(0, p)
+        statistics(0, p, factor * dot_nt(text[0:512, :], full[block(p), :]))
         return carry
 
     def column(t):
@@ -288,14 +288,15 @@
     lax.fori_loop(0, early, prev_chunk, 0)
     lax.fori_loop(early, later, own_chunk, 0)
     lax.fori_loop(early, later, prev_chunk, 0)
-    lax.fori_loop(later, PAIRS, own_chunk, 0)
 
     @pl.when(jnp.logical_not(first | last))
     def _():
+        both = arrive(PAIRS - 1, slice(0, 1024))
+        statistics(1, PAIRS - 1, both[512:1024, :])
         column(1)
         to_n.start()
-
-    lax.fori_loop(later, PAIRS, prev_chunk, 0)
+        statistics(0, PAIRS - 1, both[0:512, :])
+
     stat[4] = log_add(row_part[0], row_part[1])
     to_r.start()
     column(0)
@@ -326,11 +327,6 @@
     spread(lse_own, 512)
     to_r.wait_recv()
     row_lse[...] = log_add(stat[4], stat[5])
-    for q in range(4):
-        loss_own[q : q + 1, :] = (
-            0.5 * (row_lse[pl.ds(place[q], 1), :] + lse_own[q : q + 1, :]) - diagonal[q]
-        )
-    loss_own[4:8, :] = jnp.zeros((4, 128), F32)
     loss_copy = remote(loss_own, loss_in, L_Y, to_y)
     unit = eye.astype(F32)
 
@@ -344,13 +340,16 @@
             value = value - jnp.where(r == place[q - 4], unit, 0.0)
         prob[at, block(r, 128)] = value.astype(BF16)
 
-    def own_probability(p, carry):
-        for k in range(2):
-            for q in range(4, 8):
-                probability(p, k, q)
+    def own_probability(p, k):
+        for q in range(4, 8):
+            probability(p, k, q)
+
+    def ahead(p, carry):
+        own_probability(p, 0)
+        own_probability(p, 1)
         return carry
 
-    lax.fori_loop(0, jnp.where(first, PAIRS, 0), own_probability, 0)
+    lax.fori_loop(0, jnp.where(first, PAIRS, 0), ahead, 0)
     to_n.wait_recv()
     spread(log_add(stat[2, 0:4, :], stat[3, 0:4, :]), 0)
 
@@ -367,13 +366,18 @@
     relay_back = remote(relay_b, part_in.at[block(passed, 128)], R_A, (base, m), G_Y + passed)
 
     def prev_probability(p, carry):
-        @pl.when(jnp.logical_not(first))
-        def _():
-            own_probability(p, 0)
-
         for k in range(2):
             for q in range(4):
                 probability(p, k, q)
+        return carry
+
+    def gradient(p, carry):
+        for k in range(2):
+
+            @pl.when(jnp.logical_not(first))
+            def _():
+                own_probability(p, k)
+
             lanes = block(2 * p + k, 128)
             part_out[lanes, :] = dot_tn(prob[:, lanes], text[:, 256:512]).astype(BF16)
             if k == 0:
@@ -393,9 +397,6 @@
                     partial(2 * p + 1).start()
 
         return carry
-
-    lax.fori_loop(0, PAIRS, prev_probability, 0)
-    loss_copy.start()
 
     def visit(k):
         rows = pl.ds(256 * (k % 2), 256)
@@ -410,9 +411,27 @@
         for rows in (slice(0, 256), slice(256, 512)):
             visit_out[rows, lanes] = dot_nn(prob[rows, :], full[:, lanes]).astype(BF16)
 
+    prev_probability(0, 0)
+    gradient(0, 0)
+    lax.fori_loop(1, PAIRS, prev_probability, 0)
     visiting(1)
     visit(0).start()
     visit(1).start()
+    gradient(1, 0)
+    visiting(0)
+    visit(2).start()
+
+    @pl.when(jnp.logical_not(relay))
+    def _():
+        visit(3).start()
+
+    lax.fori_loop(2, PAIRS, gradient, 0)
+    for q in range(4):
+        loss_own[q : q + 1, :] = (
+            0.5 * (row_lse[pl.ds(place[q], 1), :] + lse_own[q : q + 1, :]) - diagonal[q]
+        )
+    loss_own[4:8, :] = jnp.zeros((4, 128), F32)
+    loss_copy.start()
 
     @pl.when(relay)
     def _():
@@ -420,13 +439,6 @@
         relay_over.start()
         partial(6).start()
         partial(7).start()
-
-    visiting(0)
-
-    @pl.when(jnp.logical_not(relay))
-    def _():
-        visit(2).start()
-        visit(3).start()
 
     def image_final(i, carry):
         late = jnp.where(i < 2, 2 * i, jnp.where(i < 6, i + 2, 2 * i - 11))
@@ -458,7 +470,6 @@
     def _():
         relay_over.wait_recv()
         relay_back.start()
-        visit(2).start()
         visit(3).start()
 
     lax.fori_loop(4, CHUNKS, image_final, 0)

time: 54.4 us -> 53.7 us (0.987)
  the two profiles are of different devices: /device:TPU:6 before, /device:TPU:8 now
where the time goes in v5:
time: 53.7 us; the launch traced here: 53.6 us
  Pallas kernels  52.3 us (97%)
  between operations  1.28 us (2%)
    pallas_call x1, Pallas kernels, local(): pl.pallas_call(functools.partial(kernel, n_dp), out_shape=(vmem((1024, 25...  50.7 us
    pallas_call x1, Pallas kernels, local(): pl.pallas_call(finish, out_shape=(jax.ShapeDtypeStruct((1024, 256), BF16)...  1.59 us

profile of v5, /device:TPU:8, one launch (start us, length us, event | category | flops | bytes accessed | tf_op | source)
XLA Modules:
  0.0 53.6 jit_solution(382461410492827705)
XLA Ops:
  1.3 50.7 %shard_map.58 = (bf16[1024,256]{1,0:T(8,128)(2,1)S(1)}, bf16[1024,256]{1,0:T(8,128)(2,1)S(1)}, f32[2,128]{1,0:T(2,128)S(1)}) custom-call(f32[1]{0:T(128)S(6)} %copy.6.factor_ref, bf16[1024,256]{1,0:T(8,128)(2,1)} %image_ref.1, bf16[1024,256]{1,0:T(8,128)(2,1)} %text_ref.1), custom_call_target="tpu_custom_call" | custom-call | flops 8589934592 | bytes 2097152 | tf_op jit(solution)/shard_map/pallas_call | solution.py:515
  52.0 1.6 %shard_map.59 = (bf16[1024,256]{1,0:T(8,128)(2,1)}, bf16[1024,256]{1,0:T(8,128)(2,1)}, f32[256]{0:T(256)}) custom-call(bf16[1024,256]{1,0:T(8,128)(2,1)S(1)} %get-tuple-element.6.image_ref, bf16[1024,256]{1,0:T(8,128)(2,1)S(1)} %get-tuple-element.7.text_ref, f32[2,128]{1,0:T(2,128)S(1)} %get-tuple-element.8.loss_ref), custom_call_target="tpu_custom_call" | custom-call | tf_op jit(solution)/shard_map/pallas_call | solution.py:559

commit v6 on v5

--- a/solution.py
+++ b/solution.py
@@ -496,7 +496,7 @@
         copy.wait_recv()
 
 
-def finish(image_ref, text_ref, loss_ref, image_out, text_out, loss_out, sem):
+def finish(image_ref, text_ref, loss_ref, image_out, text_out, loss_out, loss, sem):
     copies = []
     for k in range(4):
         rows = pl.ds(256 * k, 256)
@@ -505,7 +505,9 @@
     for copy in copies:
         copy.start()
     for k in range(2):
-        loss_out[pl.ds(128 * k, 128)] = loss_ref[k, :]
+        loss[pl.ds(128 * k, 128)] = loss_ref[k, :]
+    copies.append(pltpu.make_async_copy(loss, loss_out, sem.at[8]))
+    copies[-1].start()
     for copy in copies:
         copy.wait()
 
@@ -564,12 +566,8 @@
             jax.ShapeDtypeStruct((256,), F32),
         ),
         in_specs=[pl.BlockSpec(memory_space=vmem)] * 3,
-        out_specs=[
-            pl.BlockSpec(memory_space=pl.ANY),
-            pl.BlockSpec(memory_space=pl.ANY),
-            pl.BlockSpec(memory_space=vmem),
-        ],
-        scratch_shapes=[pltpu.SemaphoreType.DMA((8,))],
+        out_specs=[pl.BlockSpec(memory_space=pl.ANY)] * 3,
+        scratch_shapes=[vmem((256,), F32), pltpu.SemaphoreType.DMA((9,))],
     )(*(pltpu.with_memory_space_constraint(x, vmem) for x in (image_grad, text_grad, loss)))
 
 

time: 53.7 us -> 53.1 us (0.989)
    pallas_call x1, Pallas kernels: 1.59 us -> 1.04 us  [local(): pl.pallas_call(finish, out_shape=(jax.ShapeDtypeStruct((1024, 256), BF16)...]
where the time goes in v6:
time: 53.1 us; the launch traced here: 53 us
  Pallas kernels  51.8 us (98%)
  between operations  1.28 us (2%)
    pallas_call x1, Pallas kernels, local(): pl.pallas_call(functools.partial(kernel, n_dp), out_shape=(vmem((1024, 25...  50.7 us

profile of v6, /device:TPU:8, one launch (start us, length us, event | category | flops | bytes accessed | tf_op | source)
XLA Modules:
  0.0 53.0 jit_solution(9543765431275107313)
XLA Ops:
  1.3 50.7 %shard_map.58 = (bf16[1024,256]{1,0:T(8,128)(2,1)S(1)}, bf16[1024,256]{1,0:T(8,128)(2,1)S(1)}, f32[2,128]{1,0:T(2,128)S(1)}) custom-call(f32[1]{0:T(128)S(6)} %copy.6.factor_ref, bf16[1024,256]{1,0:T(8,128)(2,1)} %image_ref.1, bf16[1024,256]{1,0:T(8,128)(2,1)} %text_ref.1), custom_call_target="tpu_custom_call" | custom-call | flops 8589934592 | bytes 2097152 | tf_op jit(solution)/shard_map/pallas_call | solution.py:517
  52.0 1.0 %shard_map.59 = (bf16[1024,256]{1,0:T(8,128)(2,1)}, bf16[1024,256]{1,0:T(8,128)(2,1)}, f32[256]{0:T(256)}) custom-call(bf16[1024,256]{1,0:T(8,128)(2,1)S(1)} %get-tuple-element.6.image_ref, bf16[1024,256]{1,0:T(8,128)(2,1)S(1)} %get-tuple-element.7.text_ref, f32[2,128]{1,0:T(2,128)S(1)} %get-tuple-element.8.loss_ref), custom_call_target="tpu_custom_call" | custom-call | tf_op jit(solution)/shard_map/pallas_call | solution.py:561

commit v7 on v6

--- a/solution.py
+++ b/solution.py
@@ -371,8 +371,11 @@
                 probability(p, k, q)
         return carry
 
-    def gradient(p, carry):
+    def gradient(p, carry, with_prev=False):
         for k in range(2):
+            if with_prev:
+                for q in range(4):
+                    probability(p, k, q)
 
             @pl.when(jnp.logical_not(first))
             def _():
@@ -411,8 +414,7 @@
         for rows in (slice(0, 256), slice(256, 512)):
             visit_out[rows, lanes] = dot_nn(prob[rows, :], full[:, lanes]).astype(BF16)
 
-    prev_probability(0, 0)
-    gradient(0, 0)
+    gradient(0, 0, with_prev=True)
     lax.fori_loop(1, PAIRS, prev_probability, 0)
     visiting(1)
     visit(0).start()

time: 53.1 us -> 53.1 us (level)
  no operation moved by 1% of the time
where the time goes in v7:
time: 53.1 us; the launch traced here: 53 us
  Pallas kernels  51.7 us (97%)
  between operations  1.28 us (2%)
    pallas_call x1, Pallas kernels, local(): pl.pallas_call(functools.partial(kernel, n_dp), out_shape=(vmem((1024, 25...  50.7 us

profile of v7, /device:TPU:8, one launch (start us, length us, event | category | flops | bytes accessed | tf_op | source)
XLA Modules:
  0.0 53.0 jit_solution(15197289061621110727)
XLA Ops:
  1.3 50.7 %shard_map.58 = (bf16[1024,256]{1,0:T(8,128)(2,1)S(1)}, bf16[1024,256]{1,0:T(8,128)(2,1)S(1)}, f32[2,128]{1,0:T(2,128)S(1)}) custom-call(f32[1]{0:T(128)S(6)} %copy.6.factor_ref, bf16[1024,256]{1,0:T(8,128)(2,1)} %image_ref.1, bf16[1024,256]{1,0:T(8,128)(2,1)} %text_ref.1), custom_call_target="tpu_custom_call" | custom-call | flops 8589934592 | bytes 2097152 | tf_op jit(solution)/shard_map/pallas_call | solution.py:519
  52.0 1.0 %shard_map.59 = (bf16[1024,256]{1,0:T(8,128)(2,1)}, bf16[1024,256]{1,0:T(8,128)(2,1)}, f32[256]{0:T(256)}) custom-call(bf16[1024,256]{1,0:T(8,128)(2,1)S(1)} %get-tuple-element.6.image_ref, bf16[1024,256]{1,0:T(8,128)(2,1)S(1)} %get-tuple-element.7.text_ref, f32[2,128]{1,0:T(2,128)S(1)} %get-tuple-element.8.loss_ref), custom_call_target="tpu_custom_call" | custom-call | tf_op jit(solution)/shard_map/pallas_call | solution.py:563

commit v8 on v7

--- a/solution.py
+++ b/solution.py
@@ -499,16 +499,15 @@
 
 
 def finish(image_ref, text_ref, loss_ref, image_out, text_out, loss_out, loss, sem):
-    copies = []
-    for k in range(4):
-        rows = pl.ds(256 * k, 256)
-        copies.append(pltpu.make_async_copy(image_ref.at[rows], image_out.at[rows], sem.at[k]))
-        copies.append(pltpu.make_async_copy(text_ref.at[rows], text_out.at[rows], sem.at[4 + k]))
+    copies = [
+        pltpu.make_async_copy(image_ref, image_out, sem.at[0]),
+        pltpu.make_async_copy(text_ref, text_out, sem.at[1]),
+    ]
     for copy in copies:
         copy.start()
     for k in range(2):
         loss[pl.ds(128 * k, 128)] = loss_ref[k, :]
-    copies.append(pltpu.make_async_copy(loss, loss_out, sem.at[8]))
+    copies.append(pltpu.make_async_copy(loss, loss_out, sem.at[2]))
     copies[-1].start()
     for copy in copies:
         copy.wait()
@@ -569,7 +568,7 @@
         ),
         in_specs=[pl.BlockSpec(memory_space=vmem)] * 3,
         out_specs=[pl.BlockSpec(memory_space=pl.ANY)] * 3,
-        scratch_shapes=[vmem((256,), F32), pltpu.SemaphoreType.DMA((9,))],
+        scratch_shapes=[vmem((256,), F32), pltpu.SemaphoreType.DMA((3,))],
     )(*(pltpu.with_memory_space_constraint(x, vmem) for x in (image_grad, text_grad, loss)))
 
 

time: 53.1 us -> 53 us (level)
  no operation moved by 1% of the time
where the time goes in v8:
time: 53 us; the launch traced here: 52.9 us
  Pallas kernels  51.7 us (98%)
  between operations  1.28 us (2%)
    pallas_call x1, Pallas kernels, local(): pl.pallas_call(functools.partial(kernel, n_dp), out_shape=(vmem((1024, 25...  50.7 us

profile of v8, /device:TPU:8, one launch (start us, length us, event | category | flops | bytes accessed | tf_op | source)
XLA Modules:
  0.0 52.9 jit_solution(3220152860952923905)
XLA Ops:
  1.3 50.7 %shard_map.58 = (bf16[1024,256]{1,0:T(8,128)(2,1)S(1)}, bf16[1024,256]{1,0:T(8,128)(2,1)S(1)}, f32[2,128]{1,0:T(2,128)S(1)}) custom-call(f32[1]{0:T(128)S(6)} %copy.6.factor_ref, bf16[1024,256]{1,0:T(8,128)(2,1)} %image_ref.1, bf16[1024,256]{1,0:T(8,128)(2,1)} %text_ref.1), custom_call_target="tpu_custom_call" | custom-call | flops 8589934592 | bytes 2097152 | tf_op jit(solution)/shard_map/pallas_call | solution.py:518
  52.0 1.0 %shard_map.59 = (bf16[1024,256]{1,0:T(8,128)(2,1)}, bf16[1024,256]{1,0:T(8,128)(2,1)}, f32[256]{0:T(256)}) custom-call(bf16[1024,256]{1,0:T(8,128)(2,1)S(1)} %get-tuple-element.6.image_ref, bf16[1024,256]{1,0:T(8,128)(2,1)S(1)} %get-tuple-element.7.text_ref, f32[2,128]{1,0:T(2,128)S(1)} %get-tuple-element.8.loss_ref), custom_call_target="tpu_custom_call" | custom-call | tf_op jit(solution)/shard_map/pallas_call | solution.py:562
